TPU v7x, 32 devices: a whole 2x2x4 slice. The times are simulated.
32 devices in a mesh: fsdp: 4 (over z), context: 2 (over y), tensor: 4 (over x, core).
Axes of the slice: x: 2, y: 2, z: 4, core: 2. Of those that a mesh axis runs over, the one named last changes fastest.
Arguments:
- patches: bfloat16 [10240, 768], P(('fsdp', 'context')), may hold values from -6 to 6
- out_grad: bfloat16 [10240, 768], P(('fsdp', 'context')), may hold values from -6 to 6
- block_order: int32 [4, 20], P('fsdp'), may hold values from 0 to 19, as said below
- first_gain: float32 [768], replicated, may hold values from 0.25 to 1.75
- first_shift: float32 [768], replicated, may hold values from -2 to 2
- attn_proj: bfloat16 [3, 768, 768], P(None, 'fsdp', 'tensor'), may hold values from -0.21875 to 0.21875
- attn_bias: float32 [2, 768], P(None, 'tensor'), may hold values from -3 to 3
- out_proj: bfloat16 [768, 768], P('tensor', 'fsdp'), may hold values from -0.875 to 0.875
- out_bias: float32 [768], replicated, may hold values from -2 to 2
- second_gain: float32 [768], replicated, may hold values from 0.25 to 1.75
- second_shift: float32 [768], replicated, may hold values from -2 to 2
- up_proj: bfloat16 [768, 3072], P('fsdp', 'tensor'), may hold values from -0.21875 to 0.21875
- up_bias: float32 [3072], P('tensor'), may hold values from -3 to 3
- down_proj: bfloat16 [3072, 768], P('tensor', 'fsdp'), may hold values from -0.109375 to 0.109375
- down_bias: float32 [768], replicated, may hold values from -2 to 2
Outputs:
- result: bfloat16 [10240, 768], P(('fsdp', 'context'))
- patch_grad: float32 [10240, 768], P(('fsdp', 'context'))
- grad_first_gain: float32 [768], replicated
- grad_first_shift: float32 [768], replicated
- grad_attn_proj: float32 [3, 768, 768], P(None, 'fsdp', 'tensor')
- grad_attn_bias: float32 [2, 768], P(None, 'tensor')
- grad_out_proj: float32 [768, 768], P('tensor', 'fsdp')
- grad_out_bias: float32 [768], replicated
- grad_second_gain: float32 [768], replicated
- grad_second_shift: float32 [768], replicated
- grad_up_proj: float32 [768, 3072], P('fsdp', 'tensor')
- grad_up_bias: float32 [3072], P('tensor')
- grad_down_proj: float32 [3072, 768], P('tensor', 'fsdp')
- grad_down_bias: float32 [768], replicated
Inputs may be any that keep to these rules, and one draw needn't show every extreme that they name: `block_order`: each row lists every block number of its group once. In every group, each device of context holds 20 // 2 blocks of every tree, or one more.
All inputs are finite; a program needn't handle non-finite values.
Results may differ from a plain program's by a relative error of at most 0.0098.
Values may be sent and summed in bfloat16 or wider, within the bound.
A program may use at most 128 MiB of HBM per device.

v0:
```python
from functools import partial
import jax
import jax.numpy as jnp
from jax import lax
from jax.sharding import PartitionSpec as P

HEAD_DIM = 64
BLOCK = 128
TRUNK_BLK = 8
BRANCHES = 4
LEAVES = 2
TREE_BLK = 20
epsilon = 1e-05
far_below = -1e30


def layer_norm(values, norm_gain, norm_shift):
    center = values - jnp.mean(values, axis=1, keepdims=True)
    inverse = lax.rsqrt(jnp.mean(center * center, axis=1, keepdims=True) + epsilon)
    normed = center * inverse
    return (normed * norm_gain + norm_shift, normed, inverse)


def norm_back(gradient, normed, inverse, norm_gain):
    scaled = gradient * norm_gain
    return inverse * (
        scaled
        - jnp.mean(scaled, axis=1, keepdims=True)
        - normed * jnp.mean(scaled * normed, axis=1, keepdims=True)
    )


def slot_labels(order_row):
    position = order_row % TREE_BLK
    return (order_row // TREE_BLK, jnp.where(position < TRUNK_BLK, 0, position - TRUNK_BLK + 1))


def spread_rows(values):
    return jnp.broadcast_to(values[:, None], (values.shape[0], BLOCK)).reshape(-1)


def row_labels(labels, first_slot, slot_count):
    return tuple(
        (
            spread_rows(lax.dynamic_slice_in_dim(label_table, first_slot, slot_count))
            for label_table in labels
        )
    )


def visible(query_labels, key_labels):
    query_tree, query_seg = query_labels
    key_tree, key_seg = key_labels
    parent = jnp.where(query_seg > BRANCHES, 1 + (query_seg - BRANCHES - 1) // LEAVES, 0)
    reaches = (
        (key_seg[None, :] == 0)
        | (key_seg[None, :] == query_seg[:, None])
        | (key_seg[None, :] == parent[:, None])
    )
    return (query_tree[:, None] == key_tree[None, :]) & reaches


def head_view(matrix):
    return matrix.reshape(matrix.shape[0], matrix.shape[1] // HEAD_DIM, HEAD_DIM)


def scores_of(query_heads, key_heads):
    return jnp.einsum(
        "qhd,khd->hqk", query_heads, key_heads, preferred_element_type=jnp.float32
    ) * HEAD_DIM ** (-0.5)


def weights_of(scores, log_total, allowed):
    return jnp.where(allowed[None], jnp.exp(scores - log_total[:, :, None]), 0.0)


def score_grads(query_heads, grad_heads, key_heads, value_heads, log_total, row_delta, allowed):
    weights = weights_of(scores_of(query_heads, key_heads), log_total, allowed)
    prob_grad = jnp.einsum(
        "qhd,khd->hqk", grad_heads, value_heads, preferred_element_type=jnp.float32
    )
    return (
        (weights * (prob_grad - row_delta[:, :, None])).astype(jnp.bfloat16),
        weights.astype(jnp.bfloat16),
    )


def shards(
    patches,
    out_grad,
    block_order,
    first_gain,
    first_shift,
    attn_proj,
    attn_bias,
    out_proj,
    out_bias,
    second_gain,
    second_shift,
    up_proj,
    up_bias,
    down_proj,
    down_bias,
):
    attn_full, out_full, up_full, down_full = (
        lax.all_gather(attn_proj, "fsdp", axis=1, tiled=True),
        lax.all_gather(out_proj, "fsdp", axis=1, tiled=True),
        lax.all_gather(up_proj, "fsdp", axis=0, tiled=True),
        lax.all_gather(down_proj, "fsdp", axis=1, tiled=True),
    )
    labels = slot_labels(block_order[0])
    row_count = patches.shape[0]
    own_slots = row_count // BLOCK
    query_labels = row_labels(labels, lax.axis_index("context") * own_slots, own_slots)
    head_width = attn_full.shape[2]
    head_count = head_width // HEAD_DIM
    key_block = 4 * BLOCK
    block_slots = key_block // BLOCK
    score_scale = HEAD_DIM ** (-0.5)
    inputs = patches.astype(jnp.float32)
    first_norm, first_normed, first_inverse = layer_norm(inputs, first_gain, first_shift)
    first_low = first_norm.astype(jnp.bfloat16)
    projected = jnp.einsum("rd,cde->cre", first_low, attn_full, preferred_element_type=jnp.float32)
    queries = (projected[0] + attn_bias[0]).astype(jnp.bfloat16)
    keys_low = projected[1].astype(jnp.bfloat16)
    values_low = (projected[2] + attn_bias[1]).astype(jnp.bfloat16)
    keys_all = lax.all_gather(
        jnp.concatenate([keys_low, values_low], axis=1), "context", axis=0, tiled=True
    )
    block_count = keys_all.shape[0] // key_block
    query_heads = head_view(queries)

    def key_piece(step_index):
        key_slab = lax.dynamic_slice_in_dim(keys_all, step_index * key_block, key_block, 0)
        allowed = visible(query_labels, row_labels(labels, step_index * block_slots, block_slots))
        return (head_view(key_slab[:, :head_width]), head_view(key_slab[:, head_width:]), allowed)

    def total_step(step_index, carried):
        running_top, running_sum = carried
        key_heads, value_heads, allowed = key_piece(step_index)
        masked = jnp.where(allowed[None], scores_of(query_heads, key_heads), far_below)
        new_top = jnp.maximum(running_top, jnp.max(masked, axis=2))
        kept_exp = jnp.where(allowed[None], jnp.exp(masked - new_top[:, :, None]), 0.0)
        return (new_top, running_sum * jnp.exp(running_top - new_top) + jnp.sum(kept_exp, axis=2))

    start_top = jnp.full((head_count, row_count), far_below, jnp.float32)
    running_top, running_sum = lax.fori_loop(
        0, block_count, total_step, (start_top, jnp.zeros((head_count, row_count), jnp.float32))
    )
    log_total = running_top + jnp.log(running_sum)

    def mix_step(step_index, mixed):
        key_heads, value_heads, allowed = key_piece(step_index)
        weights = weights_of(scores_of(query_heads, key_heads), log_total, allowed).astype(
            jnp.bfloat16
        )
        return mixed + jnp.einsum(
            "hqk,khd->qhd", weights, value_heads, preferred_element_type=jnp.float32
        )

    attended = lax.fori_loop(
        0, block_count, mix_step, jnp.zeros((row_count, head_count, HEAD_DIM), jnp.float32)
    )
    attended_low = attended.reshape(row_count, head_width).astype(jnp.bfloat16)
    attn_part = jnp.dot(attended_low, out_full, preferred_element_type=jnp.float32)
    middle = inputs + (lax.psum(attn_part, "tensor") + out_bias)
    second_norm, second_normed, second_inverse = layer_norm(middle, second_gain, second_shift)
    second_low = second_norm.astype(jnp.bfloat16)
    pre_act = jnp.dot(second_low, up_full, preferred_element_type=jnp.float32) + up_bias
    hidden, gelu_back = jax.vjp(partial(jax.nn.gelu, approximate=False), pre_act)
    hidden_low = hidden.astype(jnp.bfloat16)
    mlp_part = jnp.dot(hidden_low, down_full, preferred_element_type=jnp.float32)
    result = (
        middle + (lax.psum(mlp_part.astype(jnp.bfloat16), "tensor").astype(jnp.float32) + down_bias)
    ).astype(jnp.bfloat16)
    top_grad = out_grad.astype(jnp.float32)
    grad_down_bias = jnp.sum(top_grad, axis=0)
    grad_down = jnp.einsum("rf,rd->fd", hidden_low, out_grad, preferred_element_type=jnp.float32)
    hidden_grad = jnp.einsum("rd,fd->rf", out_grad, down_full, preferred_element_type=jnp.float32)
    pre_grad = gelu_back(hidden_grad)[0].astype(jnp.bfloat16)
    grad_up_bias = jnp.sum(pre_grad.astype(jnp.float32), axis=0)
    grad_up = jnp.einsum("rd,rf->df", second_low, pre_grad, preferred_element_type=jnp.float32)
    second_part = jnp.einsum("rf,df->rd", pre_grad, up_full, preferred_element_type=jnp.float32)
    second_grad = lax.psum(second_part, "tensor")
    grad_second_gain = jnp.sum(second_grad * second_normed, axis=0)
    grad_second_shift = jnp.sum(second_grad, axis=0)
    middle_grad = top_grad + norm_back(second_grad, second_normed, second_inverse, second_gain)
    branch_grad = middle_grad.astype(jnp.bfloat16)
    grad_out_bias = jnp.sum(branch_grad.astype(jnp.float32), axis=0)
    grad_out = jnp.einsum(
        "re,rd->ed", attended_low, branch_grad, preferred_element_type=jnp.float32
    )
    attended_grad = jnp.einsum(
        "rd,ed->re", branch_grad, out_full, preferred_element_type=jnp.float32
    ).astype(jnp.bfloat16)
    grad_heads = head_view(attended_grad)

    def delta_step(step_index, row_delta):
        key_heads, value_heads, allowed = key_piece(step_index)
        weights = weights_of(scores_of(query_heads, key_heads), log_total, allowed)
        prob_grad = jnp.einsum(
            "qhd,khd->hqk", grad_heads, value_heads, preferred_element_type=jnp.float32
        )
        return row_delta + jnp.sum(weights * prob_grad, axis=2)

    row_delta = lax.fori_loop(
        0, block_count, delta_step, jnp.zeros((head_count, row_count), jnp.float32)
    )
    query_start = jnp.zeros((row_count, head_count, HEAD_DIM), jnp.float32)

    def back_step(step_index, carried):
        query_acc, key_acc = carried
        key_heads, value_heads, allowed = key_piece(step_index)
        score_low, weights_low = score_grads(
            query_heads, grad_heads, key_heads, value_heads, log_total, row_delta, allowed
        )
        query_acc = query_acc + jnp.einsum(
            "hqk,khd->qhd", score_low, key_heads, preferred_element_type=jnp.float32
        )
        key_part = jnp.einsum(
            "hqk,qhd->khd", score_low, query_heads, preferred_element_type=jnp.float32
        )
        value_part = jnp.einsum(
            "hqk,qhd->khd", weights_low, grad_heads, preferred_element_type=jnp.float32
        )
        joined = jnp.concatenate(
            [key_part.reshape(key_block, head_width), value_part.reshape(key_block, head_width)],
            axis=1,
        )
        return (
            query_acc,
            lax.dynamic_update_slice_in_dim(key_acc, joined, step_index * key_block, 0),
        )

    key_start = jnp.zeros((keys_all.shape[0], 2 * head_width), jnp.float32)
    query_acc, key_acc = lax.fori_loop(0, block_count, back_step, (query_start, key_start))
    key_value_grad = lax.psum_scatter(key_acc, "context", scatter_dimension=0, tiled=True)
    query_grad = (query_acc.reshape(row_count, head_width) * score_scale).astype(jnp.bfloat16)
    key_grad = (key_value_grad[:, :head_width] * score_scale).astype(jnp.bfloat16)
    value_grad = key_value_grad[:, head_width:].astype(jnp.bfloat16)
    stacked = jnp.stack([query_grad, key_grad, value_grad])
    grad_attn_bias = jnp.stack(
        [
            jnp.sum(query_grad.astype(jnp.float32), axis=0),
            jnp.sum(value_grad.astype(jnp.float32), axis=0),
        ]
    )
    grad_attn = jnp.einsum("rd,cre->cde", first_low, stacked, preferred_element_type=jnp.float32)
    first_grad = lax.psum(
        jnp.einsum("cre,cde->rd", stacked, attn_full, preferred_element_type=jnp.float32), "tensor"
    )
    grad_first_gain = jnp.sum(first_grad * first_normed, axis=0)
    grad_first_shift = jnp.sum(first_grad, axis=0)
    patch_grad = middle_grad + norm_back(first_grad, first_normed, first_inverse, first_gain)
    wide_attn, wide_out, wide_up, wide_down = (
        lax.psum_scatter(grad_attn, ("fsdp", "context"), scatter_dimension=1, tiled=True),
        lax.psum_scatter(grad_out, ("fsdp", "context"), scatter_dimension=1, tiled=True),
        lax.psum_scatter(grad_up, ("fsdp", "context"), scatter_dimension=0, tiled=True),
        lax.psum_scatter(grad_down, ("fsdp", "context"), scatter_dimension=1, tiled=True),
    )
    grad_attn, grad_out, grad_up, grad_down = (
        lax.all_gather(wide_attn, "context", axis=1, tiled=True),
        lax.all_gather(wide_out, "context", axis=1, tiled=True),
        lax.all_gather(wide_up, "context", axis=0, tiled=True),
        lax.all_gather(wide_down, "context", axis=1, tiled=True),
    )
    small_grads = lax.psum(
        (
            grad_first_gain,
            grad_first_shift,
            grad_attn_bias,
            grad_out_bias,
            grad_second_gain,
            grad_second_shift,
            grad_up_bias,
            grad_down_bias,
        ),
        ("fsdp", "context"),
    )
    return (
        result,
        patch_grad,
        small_grads[0],
        small_grads[1],
        grad_attn,
        small_grads[2],
        grad_out,
        small_grads[3],
        small_grads[4],
        small_grads[5],
        grad_up,
        small_grads[6],
        grad_down,
        small_grads[7],
    )


def solution(mesh):
    return jax.shard_map(
        shards,
        mesh=mesh,
        in_specs=(
            P(("fsdp", "context"), None),
            P(("fsdp", "context"), None),
            P("fsdp", None),
            P(),
            P(),
            P(None, "fsdp", "tensor"),
            P(None, "tensor"),
            P("tensor", "fsdp"),
            P(),
            P(),
            P(),
            P("fsdp", "tensor"),
            P("tensor"),
            P("tensor", "fsdp"),
            P(),
        ),
        out_specs=(
            P(("fsdp", "context"), None),
            P(("fsdp", "context"), None),
            P(),
            P(),
            P(None, "fsdp", "tensor"),
            P(None, "tensor"),
            P("tensor", "fsdp"),
            P(),
            P(),
            P(),
            P("fsdp", "tensor"),
            P("tensor"),
            P("tensor", "fsdp"),
            P(),
        ),
        check_vma=False,
    )
```

profile of v0, /device:TPU:0, one launch (start us, length us, event | category | flops | bytes accessed | tf_op | source)
XLA Modules:
  0.0 950.3 jit_solution(17451952683291024522)
XLA Ops:
  8.8 1.9 convert_reduce_fusion
  10.8 2.4 fusion.90
  13.5 31.5 %all_gather.27 = bf16[3,768,192]{2,0,1:T(4,128)(2,1)} all-gather(bf16[3,192,192]{2,0,1:T(4,128)(2,1)S(1)} %copy.39), channel_id=1, replica_groups=mesh['fsdp'=4,'context'=2,'tensor'=4] {'fsdp'}, dimensions={1}, use_global_device_ids=true | all-gather | bytes 1105920 | tf_op jit(solution)/shard_map/all_gather | solution.py:106
  45.0 2.6 copy.40
  56.9 16.8 %all_gather.29 = bf16[192,768]{0,1:T(8,128)(2,1)} all-gather(bf16[192,192]{0,1:T(8,128)(2,1)} %copy.42), channel_id=1, replica_groups=mesh['fsdp'=4,'context'=2,'tensor'=4] {'fsdp'}, dimensions={1}, use_global_device_ids=true | all-gather | bytes 368640 | tf_op jit(solution)/shard_map/all_gather | solution.py:107
  73.7 11.5 %all-gather.4.cloned.1.call-done = bf16[2560,384]{0,1:T(8,128)(2,1)} async-done(((bf16[1280,384]{0,1:T(8,128)(2,1)}), bf16[2560,384]{0,1:T(8,128)(2,1)}) %all-gather.4.cloned.1.call-update) | async-done | bytes 1966096 | tf_op jit(solution)/shard_map/all_gather | solution.py:127
  85.2 31.9 %while.88 = (s32[]{:T(128)}, f32[3,1280]{1,0:T(4,128)S(1)}, f32[3,1280]{1,0:T(4,128)S(1)}, s32[20]{0:T(128)S(1)}, s32[20]{0:T(128)S(1)}, /*index=5*/bf16[2560,38...) while((s32[]{:T(128)}, f32[3,1280]{1,0:T(4,128)S(1)}, ...), condition=%wide.region_5.6_spmd.clone.clone.clone, body=%wide.region_2.5_spmd.clone.clone.clone.sunk | while | flops 271363072 | bytes 19016176 | solution.py:147
  89.5 2.0 select_reduce_fusion.2
  95.9 2.0 select_reduce_fusion.2
  102.3 2.0 select_reduce_fusion.2
  108.7 2.0 select_reduce_fusion.2
  115.1 2.0 select_reduce_fusion.2
  117.2 40.3 %while.89 = (s32[]{:T(128)}, f32[1280,3,64]{0,2,1:T(8,128)}, bf16[2560,384]{0,1:T(8,128)(2,1)}, s32[20]{0:T(128)S(1)}, s32[20]{0:T(128)S(1)}, /*index=5*/bf16[12...) while((s32[]{:T(128)}, f32[1280,3,64]{0,2,1:T(8,128)}, ...), condition=%wide.region_7.8_spmd.clone.clone.clone, body=%wide.region_6.7_spmd.clone.clone.clone.sunk | while | flops 515629312 | bytes 5003783 | solution.py:161
  120.1 5.0 fusion.202
  127.9 5.2 fusion.202
  136.0 5.2 fusion.202
  144.1 5.2 fusion.202
  152.2 5.2 fusion.202
  159.5 3.7 fusion.123
  164.9 79.7 %all-reduce.6.cloned.1.call-done = f32[1280,768]{1,0:T(8,128)} async-done(((f32[1280,768]{1,0:T(8,128)}), f32[1280,768]{1,0:T(8,128)}) %all-reduce.6.cloned.1.call-update) | async-done | bytes 3932176 | tf_op jit(solution)/shard_map/psum | solution.py:166
  244.6 2.7 fusion.118
  249.9 6.5 convolution_add_fusion
  256.4 13.5 %convert_reduce_fusion.2 = (f32[768]{0:T(1024)}, bf16[1280,768]{1,0:T(8,128)(2,1)S(1)}, f32[1280,768]{1,0:T(8,128)}) fusion(f32[1280,768]{1,0:T(8,128)} %convolution_add_fusion, bf16[1280,768]{1,0:T(8,128)(2,1)S(1)} %copy-done.10, bf16[768,768]{0,1:T(8,128)(2,1)} %all-gather.8.cloned.1.call-done), kind=kOutput, calls=%fused_computation.149 | convolution fusion | flops 1582693632 | bytes 12979200 | tf_op jit(solution)/shard_map/rd,fd->rf/dot_general | solution.py:179
  271.2 3.7 fusion.124
  275.0 3.9 multiply_convert_fusion
  280.3 3.0 convolution_convert_fusion
  283.4 73.0 %all-reduce.10.cloned.1.call-done = f32[1280,768]{1,0:T(8,128)} async-done(((f32[1280,768]{1,0:T(8,128)}), f32[1280,768]{1,0:T(8,128)}) %all-reduce.10.cloned.1.call-update) | async-done | bytes 3932176 | tf_op jit(solution)/shard_map/psum | solution.py:184
  356.4 5.0 multiply_reduce_fusion
  361.4 47.3 %all-reduce.8.cloned.1.call-done = bf16[1280,768]{1,0:T(8,128)(2,1)} async-done(((bf16[1280,768]{1,0:T(8,128)(2,1)}), bf16[1280,768]{1,0:T(8,128)(2,1)}) %all-reduce.8.cloned.1.call-update) | async-done | bytes 1966096 | tf_op jit(solution)/shard_map/psum | solution.py:174
  408.7 5.9 convert_reduce_fusion.3
  417.3 33.9 %while.90 = (s32[]{:T(128)}, f32[3,1280]{1,0:T(4,128)S(1)}, s32[20]{0:T(128)S(1)}, s32[20]{0:T(128)S(1)}, bf16[2560,384]{0,1:T(8,128)(2,1)}, /*index=5*/bf16[128...) while((s32[]{:T(128)}, f32[3,1280]{1,0:T(4,128)S(1)}, ...), condition=%wide.region_17.18_spmd.clone.clone.clone, body=%wide.region_15.17_spmd.clone.clone.clone.sunk | while | flops 517107712 | bytes 19319308 | solution.py:206
  421.3 2.7 fusion.209
  428.0 2.7 fusion.209
  434.8 2.7 fusion.209
  441.6 2.7 fusion.209
  448.4 2.7 fusion.209
  451.1 2.4 broadcast_in_dim.438
  453.5 59.0 %while.91 = (s32[]{:T(128)}, f32[1280,3,64]{0,2,1:T(8,128)S(1)}, f32[2560,384]{0,1:T(8,128)}, bf16[2560,384]{0,1:T(8,128)(2,1)}, s32[20]{0:T(128)S(1)}, /*index=...) while((s32[]{:T(128)}, f32[1280,3,64]{0,2,1:T(8,128)S(1)}, ...), condition=%wide.region_19.20_spmd.clone.clone.clone, body=%wide.region_18.19_spmd.clone.clone.clone.sunk | while | flops 1282597120 | bytes 45109792 | solution.py:236
  459.2 2.9 fusion.223
  471.0 2.9 fusion.223
  482.8 2.9 fusion.223
  494.6 2.9 fusion.223
  506.4 2.9 fusion.223
  513.5 3.9 convolution_bitcast_fusion.3
  517.5 5.1 fusion.125
  522.7 6.4 fusion.116
  529.3 35.4 %reduce-scatter.10.cloned.1.call-done = f32[1280,384]{0,1:T(8,128)} async-done(((f32[2560,384]{0,1:T(8,128)}), f32[1280,384]{0,1:T(8,128)}) %reduce-scatter.10.cloned.1.call-update) | async-done | bytes 1966096 | tf_op jit(solution)/shard_map/reduce_scatter | solution.py:237
  567.6 3.7 convolution_bitcast_fusion.2
  572.9 2.8 fusion.99
  575.6 4.2 copy.52
  579.9 4.6 reshape.1155
  584.6 46.2 %reduce-scatter.18.cloned.1.call-done = f32[96,192]{1,0:T(8,128)} async-done(((f32[768,192]{1,0:T(8,128)}), f32[96,192]{1,0:T(8,128)}) %reduce-scatter.18.cloned.1.call-update) | async-done | bytes 73744
  630.8 5.5 all_gather.33
  637.1 65.3 %reduce-scatter.14.cloned.1.call-done = f32[768,96]{0,1:T(8,128)} async-done(((f32[768,768]{0,1:T(8,128)}), f32[768,96]{0,1:T(8,128)}) %reduce-scatter.14.cloned.1.call-update) | async-done | bytes 294928 | tf_op jit(solution)/shard_map/reduce_scatter | solution.py:259
  702.4 8.6 all_gather.35
  711.0 63.1 %reduce-scatter.12.cloned.1.call-done = f32[96,768]{1,0:T(8,128)} async-done(((f32[768,768]{1,0:T(8,128)}), f32[96,768]{1,0:T(8,128)}) %reduce-scatter.12.cloned.1.call-update) | async-done | bytes 294928 | tf_op jit(solution)/shard_map/reduce_scatter | solution.py:258
  774.1 9.6 %all_gather.34 = f32[192,768]{1,0:T(8,128)} all-gather(f32[96,768]{1,0:T(8,128)} %reduce-scatter.12.cloned.1.call-done), channel_id=1, replica_groups=mesh['fsdp'=4,'context'=2,'tensor'=4] {'context'}, dimensions={0}, use_global_device_ids=true | all-gather | bytes 884736 | tf_op jit(solution)/shard_map/all_gather | solution.py:264
  783.8 73.6 %all-reduce.12.cloned.1.call-done = f32[1280,768]{1,0:T(8,128)} async-done(((f32[1280,768]{1,0:T(8,128)}), f32[1280,768]{1,0:T(8,128)}) %all-reduce.12.cloned.1.call-update) | async-done | bytes 3932176 | tf_op jit(solution)/shard_map/psum | solution.py:249
  857.4 3.5 fusion.89
  860.9 38.0 %all-reduce = (f32[768]{0:T(1024)}, f32[768]{0:T(1024)}, f32[2,192]{1,0:T(2,128)}, f32[768]{0:T(1024)}, f32[768]{0:T(1024)}, /*index=5*/f32[768]{0:T(1024)}, f32[768]{0:T(1024)}, f32[768]{0:T(1024)}) all-reduce(f32[768]{0:T(1024)S(1)} %get-tuple-element.1970, ...), channel_id=1, replica_groups=mesh['fsdp'=4,'context'=2,'tensor'=4] {'fsdp','context'}, use_global_device_ids=true, to_apply=%region_25.26 | all-reduce | flops 5760 | bytes 46080 | tf_op jit(solution)/shard_map/psum | solution.py:267
  899.0 5.4 fusion.88
  904.3 23.6 %reduce-scatter.16.cloned.1.call-done = f32[96,576]{1,0:T(8,128)} async-done(((f32[768,576]{1,0:T(8,128)}), f32[96,576]{1,0:T(8,128)}) %reduce-scatter.16.cloned.1.call-update) | async-done | bytes 221200
  929.0 9.8 %all_gather.32 = f32[3,192,192]{2,0,1:T(4,128)S(1)} all-gather(f32[3,96,192]{2,0,1:T(4,128)S(1)} %bitcast.417), channel_id=1, replica_groups=mesh['fsdp'=4,'context'=2,'tensor'=4] {'context'}, dimensions={1}, use_global_device_ids=true | all-gather | bytes 663552 | tf_op jit(solution)/shard_map/all_gather | solution.py:262
  939.7 1.9 copy.98
  (350 shorter events, 131.3 us)
Async XLA Ops:
  8.0 5.2 copy-start.13
  8.0 77.2 %all-gather.4.cloned.1.call-start = ((), (), s32[]{:S(2)}) async-start(), calls=%async_computation.5 | async-start | bytes 2949120 | tf_op jit(solution)/shard_map/all_gather | solution.py:127
  10.7 36.9 %copy-start.2 = (bf16[1280,768]{1,0:T(8,128)(2,1)S(1)}, bf16[1280,768]{1,0:T(8,128)(2,1)}, u32[]{:S(2)}) copy-start(bf16[1280,768]{1,0:T(8,128)(2,1)} %param.23) | copy-start | bytes 5898244
  10.7 36.9 %copy-start.18 = (f32[768]{0:T(1024)S(1)}, f32[768]{0:T(1024)}, u32[]{:S(2)}) copy-start(f32[768]{0:T(1024)} %param.26) | copy-start | bytes 9220
  10.7 36.9 %copy-start.31 = (f32[768]{0:T(1024)S(1)}, f32[768]{0:T(1024)}, u32[]{:S(2)}) copy-start(f32[768]{0:T(1024)} %param.27) | copy-start | bytes 9220
  10.8 38.4 %copy-start.14 = (f32[1280]{0:T(1024)}, f32[1280]{0:T(1024)S(1)}, u32[]{:S(2)}) copy-start(f32[1280]{0:T(1024)S(1)} %broadcast_multiply_fusion.5) | copy-start | bytes 15364
  13.2 36.0 %copy-start.16 = (f32[1280]{0:T(1024)}, f32[1280]{0:T(1024)S(1)}, u32[]{:S(2)}) copy-start(f32[1280]{0:T(1024)S(1)} %add_rsqrt_fusion.1) | copy-start | bytes 15364
  47.6 1.6 copy-start.11
  49.2 1.6 copy-start.7
  49.2 4.2 copy-start.33
  52.0 192.6 %all-reduce.6.cloned.1.call-start = ((), (), s32[]{:S(2)}) async-start(), calls=%async_computation.6 | async-start | bytes 7864320 | tf_op jit(solution)/shard_map/psum | solution.py:166
  158.7 0.8 copy-start.4
  159.5 85.1 %copy-start.23 = (f32[768]{0:T(1024)S(1)}, f32[768]{0:T(1024)}, u32[]{:S(2)}) copy-start(f32[768]{0:T(1024)} %param.31) | copy-start | bytes 9220
  163.2 86.7 %all-gather.6.cloned.1.call-start = ((), (), s32[]{:S(2)}) async-start(), calls=%async_computation.7 | async-start | bytes 1474560 | tf_op jit(solution)/shard_map/all_gather | solution.py:108
  163.8 92.7 %all-gather.8.cloned.1.call-start = ((), (), s32[]{:S(2)}) async-start(), calls=%async_computation.8 | async-start | bytes 1474560 | tf_op jit(solution)/shard_map/all_gather | solution.py:109
  164.4 192.1 %all-reduce.10.cloned.1.call-start = ((), (), s32[]{:S(2)}) async-start(), calls=%async_computation.10 | async-start | bytes 7864320 | tf_op jit(solution)/shard_map/psum | solution.py:184
  247.3 1.9 copy-start.1
  247.3 2.6 copy-start.20
  247.3 2.6 copy-start.28
  247.3 2.6 copy-start.29
  249.8 6.6 copy-start.10
  256.4 14.8 %copy-start.27 = (bf16[768,768]{1,0:T(8,128)(2,1)S(1)}, bf16[768,768]{1,0:T(8,128)(2,1)}, u32[]{:S(2)}) copy-start(bf16[768,768]{1,0:T(8,128)(2,1)} %all-gather.6.cloned.1.call-done) | copy-start | bytes 3538948
  269.9 1.3 copy-start.34
  274.9 133.8 %all-reduce.8.cloned.1.call-start = ((), (), s32[]{:S(2)}) async-start(), calls=%async_computation.9 | async-start | bytes 3932160 | tf_op jit(solution)/shard_map/psum | solution.py:174
  275.0 5.3 copy-start.26
  278.9 1.4 copy-start.8
  283.3 281.4 %reduce-scatter.10.cloned.1.call-start = ((), (), s32[]{:S(2)}) async-start(), calls=%async_computation.11 | async-start | bytes 5898240 | tf_op jit(solution)/shard_map/reduce_scatter | solution.py:237
  283.4 125.3 %copy-start.24 = (f32[768]{0:T(1024)S(1)}, f32[768]{0:T(1024)}, u32[]{:S(2)}) copy-start(f32[768]{0:T(1024)} %param.37) | copy-start | bytes 9220
  408.7 7.8 copy-start.6
  414.6 1.9 copy-start
  512.5 1.0 copy-start.5
  512.5 5.0 copy-start.9
  512.5 118.2 %reduce-scatter.18.cloned.1.call-start = ((), (), s32[]{:S(2)}) async-start(), calls=%async_computation.16 | async-start | bytes 884736
  517.4 5.3 copy-start.30
  517.5 184.9 %reduce-scatter.14.cloned.1.call-start = ((), (), s32[]{:S(2)}) async-start(), calls=%async_computation.14 | async-start | bytes 2654208 | tf_op jit(solution)/shard_map/reduce_scatter | solution.py:259
  522.7 251.5 %reduce-scatter.12.cloned.1.call-start = ((), (), s32[]{:S(2)}) async-start(), calls=%async_computation.13 | async-start | bytes 2654208 | tf_op jit(solution)/shard_map/reduce_scatter | solution.py:258
  529.1 38.5 %copy-start.12 = (bf16[3,768,192]{1,2,0:T(8,128)(2,1)S(1)}, bf16[3,768,192]{1,2,0:T(8,128)(2,1)}, u32[]{:S(2)}) copy-start(bf16[3,768,192]{1,2,0:T(8,128)(2,1)} %copy-done.11) | copy-start | bytes 2654212
  529.1 328.2 %all-reduce.12.cloned.1.call-start = ((), (), s32[]{:S(2)}) async-start(), calls=%async_computation.12 | async-start | bytes 7864320 | tf_op jit(solution)/shard_map/psum | solution.py:249
  571.3 1.5 copy-start.3
  571.3 1.5 copy-start.15
  571.3 1.5 copy-start.17
  571.3 1.5 copy-start.19
  571.3 1.5 copy-start.32
  571.3 356.5 %reduce-scatter.16.cloned.1.call-start = ((), (), s32[]{:S(2)}) async-start(), calls=%async_computation.15 | async-start | bytes 2211840
  637.1 223.8 %copy-start.21 = (f32[768]{0:T(1024)S(1)}, f32[768]{0:T(1024)}, u32[]{:S(2)}) copy-start(f32[768]{0:T(1024)} %get-tuple-element.1968) | copy-start | bytes 9220
  637.1 223.8 %copy-start.22 = (f32[768]{0:T(1024)S(1)}, f32[768]{0:T(1024)}, u32[]{:S(2)}) copy-start(f32[768]{0:T(1024)} %get-tuple-element.1974) | copy-start | bytes 9220
  637.1 223.9 %copy-start.25 = (f32[768]{0:T(1024)S(1)}, f32[768]{0:T(1024)}, u32[]{:S(2)}) copy-start(f32[768]{0:T(1024)} %get-tuple-element.2064) | copy-start | bytes 9220
Sparse Core Ops, SparseCore 0:
  52.1 33.0 all-gather.3
  163.3 81.2 all-reduce.5
  275.0 81.3 all-reduce.9
  359.2 49.3 all-reduce.7
  512.6 52.0 reduce-scatter.9
  568.3 62.4 reduce-scatter.17
  634.3 68.0 reduce-scatter.13
  705.9 68.1 reduce-scatter.11
  777.1 80.2 all-reduce.11
  860.7 67.1 reduce-scatter.15
Sparse Core Ops, SparseCore 1:
  165.2 30.2 all-gather.5
  196.9 29.4 all-gather.7
where the time goes:
time: 960 us; the launch traced here: 950 us
  waiting for transfers between devices  520 us (54%)
  matrix products  149 us (16%)
  blocking collectives  120 us (12%)
  other arithmetic  79.5 us (8%)
  local copies, waits for them, and re-layouts  63.7 us (7%)
  between operations  16.6 us (2%)
    psum x1, waiting for transfers between devices, shards(): middle = inputs + (lax.psum(attn_part, 'tensor') + out_bias)  79.7 us
    psum x1, waiting for transfers between devices, shards(): lax.psum(jnp.einsum('cre,cde->rd', stacked, attn_full, preferred_element_...  73.6 us
    psum x1, waiting for transfers between devices, shards(): second_grad = lax.psum(second_part, 'tensor')  73 us
    unnamed x14, waiting for transfers between devices  70.9 us
    reduce_scatter x1, waiting for transfers between devices, shards(): lax.psum_scatter(grad_down, ('fsdp', 'context'), scatter_dimension=1, til...  65.3 us
    reduce_scatter x1, waiting for transfers between devices, shards(): lax.psum_scatter(grad_up, ('fsdp', 'context'), scatter_dimension=0, tiled...  63.1 us
    psum x1, waiting for transfers between devices, shards(): lax.psum(mlp_part.astype(jnp.bfloat16), 'tensor').astype(jnp.float32)  47.3 us
    psum x1, blocking collectives, shards(): lax.psum((grad_first_gain, grad_first_shift, grad_attn_bias, grad_out_bia...  38 us
  transfers between devices with their start and end apart: 12, of which 10 were waited for; matrix products, arithmetic and copies ran while one was open for 7% of the time, Pallas kernels for 0%

commit v1 on v0

--- a/solution.py
+++ b/solution.py
@@ -246,9 +246,9 @@
         ]
     )
     grad_attn = jnp.einsum("rd,cre->cde", first_low, stacked, preferred_element_type=jnp.float32)
-    first_grad = lax.psum(
-        jnp.einsum("cre,cde->rd", stacked, attn_full, preferred_element_type=jnp.float32), "tensor"
-    )
+    part = jnp.einsum("cre,cde->rd", stacked, attn_full, preferred_element_type=jnp.float32)
+    parts = lax.all_gather(part, "tensor", axis=0, tiled=False)
+    first_grad = parts.sum(axis=0)
     grad_first_gain = jnp.sum(first_grad * first_normed, axis=0)
     grad_first_shift = jnp.sum(first_grad, axis=0)
     patch_grad = middle_grad + norm_back(first_grad, first_normed, first_inverse, first_gain)

time: 960 us -> 1030 us (1.073)
  waiting for transfers between devices: 520 us -> 571 us
  other arithmetic: 79.5 us -> 94.3 us
    all_gather x0 -> x1, waiting for transfers between devices: none -> 88.8 us  [shards(): parts = lax.all_gather(part, 'tensor', axis=0, tiled=False)]
    psum x1 -> x0, waiting for transfers between devices: 73.6 us -> none  [shards(): lax.psum(jnp.einsum('cre,cde->rd', stacked, attn_full, preferred_element_...]
    unnamed x14, waiting for transfers between devices: 70.9 us -> 107 us
    reduce_sum x0 -> x2, other arithmetic: none -> 15.3 us  [the longest x1 8.92 us: shards(): first_grad = parts.sum(axis=0)]
    unnamed x80 -> x92, local copies, waits for them, and re-layouts: 28.8 us -> 27.1 us
  transfers between devices with their start and end apart: 12 -> 12, of which waited for: 10 -> 10; matrix products, arithmetic and copies ran while one was open for 7% -> 6% of each run, Pallas kernels for 0% -> 0%
where the time goes in v1:
time: 1030 us; the launch traced here: 1020 us
  waiting for transfers between devices  571 us (55%)
  matrix products  150 us (15%)
  blocking collectives  120 us (12%)
  other arithmetic  94.3 us (9%)
  local copies, waits for them, and re-layouts  62.1 us (6%)
  between operations  16.5 us (2%)
    unnamed x14, waiting for transfers between devices  107 us
    all_gather x1, waiting for transfers between devices, shards(): parts = lax.all_gather(part, 'tensor', axis=0, tiled=False)  88.8 us
    psum x1, waiting for transfers between devices, shards(): middle = inputs + (lax.psum(attn_part, 'tensor') + out_bias)  80 us
    psum x1, waiting for transfers between devices, shards(): second_grad = lax.psum(second_part, 'tensor')  73.1 us
    reduce_scatter x1, waiting for transfers between devices, shards(): lax.psum_scatter(grad_down, ('fsdp', 'context'), scatter_dimension=1, til...  65.4 us
    reduce_scatter x1, waiting for transfers between devices, shards(): lax.psum_scatter(grad_up, ('fsdp', 'context'), scatter_dimension=0, tiled...  63.1 us
    psum x1, waiting for transfers between devices, shards(): lax.psum(mlp_part.astype(jnp.bfloat16), 'tensor').astype(jnp.float32)  47.2 us
    psum x1, blocking collectives, shards(): lax.psum((grad_first_gain, grad_first_shift, grad_attn_bias, grad_out_bia...  37.7 us
  transfers between devices with their start and end apart: 12, of which 10 were waited for; matrix products, arithmetic and copies ran while one was open for 6% of the time, Pallas kernels for 0%

profile of v1, /device:TPU:0, one launch (start us, length us, event | category | flops | bytes accessed | tf_op | source)
XLA Modules:
  0.0 1015.5 jit_solution(12448731424534735921)
XLA Ops:
  10.8 2.4 fusion.90
  13.5 31.5 %all_gather.33 = bf16[3,768,192]{2,0,1:T(4,128)(2,1)} all-gather(bf16[3,192,192]{2,0,1:T(4,128)(2,1)S(1)} %copy.39), channel_id=1, replica_groups=mesh['fsdp'=4,'context'=2,'tensor'=4] {'fsdp'}, dimensions={1}, use_global_device_ids=true | all-gather | bytes 1105920 | tf_op jit(solution)/shard_map/all_gather | solution.py:106
  45.0 2.6 copy.40
  56.9 16.8 %all_gather.35 = bf16[192,768]{0,1:T(8,128)(2,1)} all-gather(bf16[192,192]{0,1:T(8,128)(2,1)} %copy.42), channel_id=1, replica_groups=mesh['fsdp'=4,'context'=2,'tensor'=4] {'fsdp'}, dimensions={1}, use_global_device_ids=true | all-gather | bytes 368640 | tf_op jit(solution)/shard_map/all_gather | solution.py:107
  73.8 11.5 %all-gather.6.cloned.1.call-done = bf16[2560,384]{0,1:T(8,128)(2,1)} async-done(((bf16[1280,384]{0,1:T(8,128)(2,1)}), bf16[2560,384]{0,1:T(8,128)(2,1)}) %all-gather.6.cloned.1.call-update) | async-done | bytes 1966096 | tf_op jit(solution)/shard_map/all_gather | solution.py:127
  85.2 31.9 %while.88 = (s32[]{:T(128)}, f32[3,1280]{1,0:T(4,128)S(1)}, f32[3,1280]{1,0:T(4,128)S(1)}, s32[20]{0:T(128)S(1)}, s32[20]{0:T(128)S(1)}, /*index=5*/bf16[2560,38...) while((s32[]{:T(128)}, f32[3,1280]{1,0:T(4,128)S(1)}, ...), condition=%wide.region_5.6_spmd.clone.clone.clone, body=%wide.region_2.5_spmd.clone.clone.clone.sunk | while | flops 271363072 | bytes 19016176 | solution.py:147
  89.5 2.0 select_reduce_fusion.2
  95.9 2.0 select_reduce_fusion.2
  102.3 2.0 select_reduce_fusion.2
  108.7 2.0 select_reduce_fusion.2
  115.1 2.0 select_reduce_fusion.2
  117.2 40.2 %while.89 = (s32[]{:T(128)}, f32[1280,3,64]{0,2,1:T(8,128)}, bf16[2560,384]{0,1:T(8,128)(2,1)}, s32[20]{0:T(128)S(1)}, s32[20]{0:T(128)S(1)}, /*index=5*/bf16[12...) while((s32[]{:T(128)}, f32[1280,3,64]{0,2,1:T(8,128)}, ...), condition=%wide.region_7.8_spmd.clone.clone.clone, body=%wide.region_6.7_spmd.clone.clone.clone.sunk | while | flops 515629312 | bytes 5003783 | solution.py:161
  120.1 5.0 fusion.202
  127.9 5.2 fusion.202
  136.0 5.2 fusion.202
  144.1 5.2 fusion.202
  152.2 5.2 fusion.202
  159.4 3.7 fusion.123
  164.5 80.0 %all-reduce.5.cloned.1.call-done = f32[1280,768]{1,0:T(8,128)} async-done(((f32[1280,768]{1,0:T(8,128)}), f32[1280,768]{1,0:T(8,128)}) %all-reduce.5.cloned.1.call-update) | async-done | bytes 3932176 | tf_op jit(solution)/shard_map/psum | solution.py:166
  244.5 2.7 fusion.118
  249.8 6.5 convolution_add_fusion
  256.4 13.5 %convert_reduce_fusion.2 = (f32[768]{0:T(1024)}, bf16[1280,768]{1,0:T(8,128)(2,1)S(1)}, f32[1280,768]{1,0:T(8,128)}) fusion(f32[1280,768]{1,0:T(8,128)} %convolution_add_fusion, bf16[1280,768]{1,0:T(8,128)(2,1)S(1)} %copy-done.12, bf16[768,768]{0,1:T(8,128)(2,1)} %all-gather.10.cloned.1.call-done), kind=kOutput, calls=%fused_computation.149 | convolution fusion | flops 1582693632 | bytes 12979200 | tf_op jit(solution)/shard_map/rd,fd->rf/dot_general | solution.py:179
  271.2 3.7 fusion.124
  275.0 3.9 multiply_convert_fusion
  280.2 3.0 convolution_convert_fusion
  283.4 73.1 %all-reduce.9.cloned.1.call-done = f32[1280,768]{1,0:T(8,128)} async-done(((f32[1280,768]{1,0:T(8,128)}), f32[1280,768]{1,0:T(8,128)}) %all-reduce.9.cloned.1.call-update) | async-done | bytes 3932176 | tf_op jit(solution)/shard_map/psum | solution.py:184
  356.4 5.0 multiply_reduce_fusion
  361.4 47.2 %all-reduce.7.cloned.1.call-done = bf16[1280,768]{1,0:T(8,128)(2,1)} async-done(((bf16[1280,768]{1,0:T(8,128)(2,1)}), bf16[1280,768]{1,0:T(8,128)(2,1)}) %all-reduce.7.cloned.1.call-update) | async-done | bytes 1966096 | tf_op jit(solution)/shard_map/psum | solution.py:174
  408.7 6.5 convert_reduce_fusion.3
  417.9 33.9 %while.90 = (s32[]{:T(128)}, f32[3,1280]{1,0:T(4,128)S(1)}, s32[20]{0:T(128)S(1)}, s32[20]{0:T(128)S(1)}, bf16[2560,384]{0,1:T(8,128)(2,1)}, /*index=5*/bf16[128...) while((s32[]{:T(128)}, f32[3,1280]{1,0:T(4,128)S(1)}, ...), condition=%wide.region_17.18_spmd.clone.clone.clone, body=%wide.region_15.17_spmd.clone.clone.clone.sunk | while | flops 517107712 | bytes 19319308 | solution.py:206
  421.9 2.7 fusion.209
  428.7 2.7 fusion.209
  435.4 2.7 fusion.209
  442.2 2.7 fusion.209
  449.0 2.7 fusion.209
  451.8 2.3 broadcast_in_dim.438
  454.1 59.0 %while.91 = (s32[]{:T(128)}, f32[1280,3,64]{0,2,1:T(8,128)S(1)}, f32[2560,384]{0,1:T(8,128)}, bf16[2560,384]{0,1:T(8,128)(2,1)}, s32[20]{0:T(128)S(1)}, /*index=...) while((s32[]{:T(128)}, f32[1280,3,64]{0,2,1:T(8,128)S(1)}, ...), condition=%wide.region_19.20_spmd.clone.clone.clone, body=%wide.region_18.19_spmd.clone.clone.clone.sunk | while | flops 1282597120 | bytes 45109792 | solution.py:236
  459.8 2.9 fusion.223
  471.7 2.9 fusion.223
  483.5 2.9 fusion.223
  495.3 2.9 fusion.223
  507.1 2.9 fusion.223
  514.1 3.9 convolution_bitcast_fusion.3
  518.1 5.2 fusion.125
  523.4 6.3 fusion.116
  529.9 35.4 %reduce-scatter.10.cloned.1.call-done = f32[1280,384]{0,1:T(8,128)} async-done(((f32[2560,384]{0,1:T(8,128)}), f32[1280,384]{0,1:T(8,128)}) %reduce-scatter.10.cloned.1.call-update) | async-done | bytes 1966096 | tf_op jit(solution)/shard_map/reduce_scatter | solution.py:237
  569.2 2.8 fusion.99
  572.1 4.2 copy.52
  576.3 4.7 reshape.1156
  581.1 4.8 convolution_bitcast_fusion.2
  586.0 45.4 %reduce-scatter.18.cloned.1.call-done = f32[96,192]{1,0:T(8,128)} async-done(((f32[768,192]{1,0:T(8,128)}), f32[96,192]{1,0:T(8,128)}) %reduce-scatter.18.cloned.1.call-update) | async-done | bytes 73744
  631.4 5.5 all_gather.41
  637.7 65.4 %reduce-scatter.14.cloned.1.call-done = f32[768,96]{0,1:T(8,128)} async-done(((f32[768,768]{0,1:T(8,128)}), f32[768,96]{0,1:T(8,128)}) %reduce-scatter.14.cloned.1.call-update) | async-done | bytes 294928 | tf_op jit(solution)/shard_map/reduce_scatter | solution.py:259
  703.1 8.6 all_gather.43
  711.7 63.1 %reduce-scatter.12.cloned.1.call-done = f32[96,768]{1,0:T(8,128)} async-done(((f32[768,768]{1,0:T(8,128)}), f32[96,768]{1,0:T(8,128)}) %reduce-scatter.12.cloned.1.call-update) | async-done | bytes 294928 | tf_op jit(solution)/shard_map/reduce_scatter | solution.py:258
  774.8 9.6 all_gather.42
  784.4 60.0 %reduce-scatter.16.cloned.1.call-done = f32[96,576]{1,0:T(8,128)} async-done(((f32[768,576]{1,0:T(8,128)}), f32[96,576]{1,0:T(8,128)}) %reduce-scatter.16.cloned.1.call-update) | async-done | bytes 221200
  845.5 10.1 all_gather.40
  856.6 88.8 %all-gather.12.cloned.1.call-done = f32[5120,768]{1,0:T(8,128)} async-done(((f32[1280,768]{1,0:T(8,128)}), f32[5120,768]{1,0:T(8,128)}) %all-gather.12.cloned.1.call-update) | async-done | bytes 15728656 | tf_op jit(solution)/shard_map/all_gather | solution.py:250
  945.3 8.9 reduce_sum.208
  954.3 3.5 fusion.89
  957.8 4.3 fusion.88
  962.2 6.4 reduce_sum.212
  968.6 37.7 %all-reduce = (f32[768]{0:T(1024)}, f32[768]{0:T(1024)}, f32[2,192]{1,0:T(2,128)}, f32[768]{0:T(1024)}, f32[768]{0:T(1024)}, /*index=5*/f32[768]{0:T(1024)}, f32[768]{0:T(1024)}, f32[768]{0:T(1024)}) all-reduce(f32[768]{0:T(1024)S(1)} %get-tuple-element.1970, ...), channel_id=1, replica_groups=mesh['fsdp'=4,'context'=2,'tensor'=4] {'fsdp','context'}, use_global_device_ids=true, to_apply=%region_25.26 | all-reduce | flops 5760 | bytes 46080 | tf_op jit(solution)/shard_map/psum | solution.py:267
  (364 shorter events, 133.3 us)
Async XLA Ops:
  8.0 5.2 copy-start.17
  8.0 77.2 %all-gather.6.cloned.1.call-start = ((), (), s32[]{:S(2)}) async-start(), calls=%async_computation.5 | async-start | bytes 2949120 | tf_op jit(solution)/shard_map/all_gather | solution.py:127
  10.7 36.9 %copy-start.3 = (bf16[1280,768]{1,0:T(8,128)(2,1)S(1)}, bf16[1280,768]{1,0:T(8,128)(2,1)}, u32[]{:S(2)}) copy-start(bf16[1280,768]{1,0:T(8,128)(2,1)} %param.23) | copy-start | bytes 5898244
  10.7 36.9 %copy-start.22 = (f32[768]{0:T(1024)S(1)}, f32[768]{0:T(1024)}, u32[]{:S(2)}) copy-start(f32[768]{0:T(1024)} %param.26) | copy-start | bytes 9220
  10.7 36.9 %copy-start.37 = (f32[768]{0:T(1024)S(1)}, f32[768]{0:T(1024)}, u32[]{:S(2)}) copy-start(f32[768]{0:T(1024)} %param.27) | copy-start | bytes 9220
  10.8 38.4 %copy-start.18 = (f32[1280]{0:T(1024)}, f32[1280]{0:T(1024)S(1)}, u32[]{:S(2)}) copy-start(f32[1280]{0:T(1024)S(1)} %broadcast_multiply_fusion.5) | copy-start | bytes 15364
  13.2 36.0 %copy-start.20 = (f32[1280]{0:T(1024)}, f32[1280]{0:T(1024)S(1)}, u32[]{:S(2)}) copy-start(f32[1280]{0:T(1024)S(1)} %add_rsqrt_fusion.1) | copy-start | bytes 15364
  47.6 1.6 copy-start.13
  49.2 1.6 copy-start.9
  49.2 4.2 copy-start.39
  52.0 192.5 %all-reduce.5.cloned.1.call-start = ((), (), s32[]{:S(2)}) async-start(), calls=%async_computation.6 | async-start | bytes 7864320 | tf_op jit(solution)/shard_map/psum | solution.py:166
  158.7 0.8 copy-start.5
  159.4 85.1 %copy-start.29 = (f32[768]{0:T(1024)S(1)}, f32[768]{0:T(1024)}, u32[]{:S(2)}) copy-start(f32[768]{0:T(1024)} %param.31) | copy-start | bytes 9220
  163.1 86.7 %all-gather.8.cloned.1.call-start = ((), (), s32[]{:S(2)}) async-start(), calls=%async_computation.7 | async-start | bytes 1474560 | tf_op jit(solution)/shard_map/all_gather | solution.py:108
  163.7 92.6 %all-gather.10.cloned.1.call-start = ((), (), s32[]{:S(2)}) async-start(), calls=%async_computation.8 | async-start | bytes 1474560 | tf_op jit(solution)/shard_map/all_gather | solution.py:109
  164.3 192.1 %all-reduce.9.cloned.1.call-start = ((), (), s32[]{:S(2)}) async-start(), calls=%async_computation.10 | async-start | bytes 7864320 | tf_op jit(solution)/shard_map/psum | solution.py:184
  247.2 1.9 copy-start.2
  247.2 2.6 copy-start.24
  247.2 2.6 copy-start.34
  247.3 2.6 copy-start.35
  249.7 6.6 copy-start.12
  256.4 14.9 %copy-start.33 = (bf16[768,768]{1,0:T(8,128)(2,1)S(1)}, bf16[768,768]{1,0:T(8,128)(2,1)}, u32[]{:S(2)}) copy-start(bf16[768,768]{1,0:T(8,128)(2,1)} %all-gather.8.cloned.1.call-done) | copy-start | bytes 3538948
  269.9 1.4 copy-start.40
  274.9 133.8 %all-reduce.7.cloned.1.call-start = ((), (), s32[]{:S(2)}) async-start(), calls=%async_computation.9 | async-start | bytes 3932160 | tf_op jit(solution)/shard_map/psum | solution.py:174
  274.9 5.3 copy-start.32
  278.9 1.3 copy-start.10
  283.3 282.1 %reduce-scatter.10.cloned.1.call-start = ((), (), s32[]{:S(2)}) async-start(), calls=%async_computation.11 | async-start | bytes 5898240 | tf_op jit(solution)/shard_map/reduce_scatter | solution.py:237
  283.4 125.3 %copy-start.30 = (f32[768]{0:T(1024)S(1)}, f32[768]{0:T(1024)}, u32[]{:S(2)}) copy-start(f32[768]{0:T(1024)} %param.37) | copy-start | bytes 9220
  408.7 8.4 copy-start.7
  415.2 1.9 copy-start
  513.1 1.0 copy-start.6
  513.1 5.0 copy-start.11
  513.1 118.3 %reduce-scatter.18.cloned.1.call-start = ((), (), s32[]{:S(2)}) async-start(), calls=%async_computation.16 | async-start | bytes 884736
  518.1 5.3 copy-start.36
  518.1 185.0 %reduce-scatter.14.cloned.1.call-start = ((), (), s32[]{:S(2)}) async-start(), calls=%async_computation.13 | async-start | bytes 2654208 | tf_op jit(solution)/shard_map/reduce_scatter | solution.py:259
  523.3 251.5 %reduce-scatter.12.cloned.1.call-start = ((), (), s32[]{:S(2)}) async-start(), calls=%async_computation.12 | async-start | bytes 2654208 | tf_op jit(solution)/shard_map/reduce_scatter | solution.py:258
  529.7 39.5 %copy-start.4 = (bf16[1280,768]{1,0:T(8,128)(2,1)S(1)}, bf16[1280,768]{1,0:T(8,128)(2,1)}, u32[]{:S(2)}) copy-start(bf16[1280,768]{1,0:T(8,128)(2,1)} %param.23) | copy-start | bytes 5898244
  529.7 39.5 %copy-start.19 = (f32[1280]{0:T(1024)S(1)}, f32[1280]{0:T(1024)}, u32[]{:S(2)}) copy-start(f32[1280]{0:T(1024)} %copy-done.18) | copy-start | bytes 15364
  529.7 39.5 %copy-start.21 = (f32[1280]{0:T(1024)S(1)}, f32[1280]{0:T(1024)}, u32[]{:S(2)}) copy-start(f32[1280]{0:T(1024)} %copy-done.20) | copy-start | bytes 15364
  529.7 39.5 %copy-start.23 = (f32[768]{0:T(1024)S(1)}, f32[768]{0:T(1024)}, u32[]{:S(2)}) copy-start(f32[768]{0:T(1024)} %param.26) | copy-start | bytes 9220
  529.7 39.5 %copy-start.38 = (f32[768]{0:T(1024)S(1)}, f32[768]{0:T(1024)}, u32[]{:S(2)}) copy-start(f32[768]{0:T(1024)} %param.27) | copy-start | bytes 9220
  529.7 314.7 %reduce-scatter.16.cloned.1.call-start = ((), (), s32[]{:S(2)}) async-start(), calls=%async_computation.15 | async-start | bytes 2211840
  567.0 1.5 copy-start.15
  568.4 0.8 copy-start.16
  576.3 4.8 copy-start.14
  581.0 364.3 %all-gather.12.cloned.1.call-start = ((), (), s32[]{:S(2)}) async-start(), calls=%async_computation.14 | async-start | bytes 19660800 | tf_op jit(solution)/shard_map/all_gather | solution.py:250
  954.3 3.6 copy-start.1
  962.1 6.4 copy-start.25
  962.1 6.4 copy-start.26
  962.1 6.4 copy-start.27
  962.1 6.4 copy-start.28
  962.1 6.4 copy-start.31
  962.1 44.1 %copy-start.8 = (f32[192,768]{1,0:T(8,128)S(1)}, f32[192,768]{1,0:T(8,128)}, u32[]{:S(2)}) copy-start(f32[192,768]{1,0:T(8,128)} %all_gather.42) | copy-start | bytes 1769476
Sparse Core Ops, SparseCore 0:
  52.1 33.0 all-gather.5
  163.2 81.2 all-reduce.4
  275.0 81.3 all-reduce.8
  359.2 49.3 all-reduce.6
  513.3 52.0 reduce-scatter.9
  568.9 62.5 reduce-scatter.17
  634.9 68.1 reduce-scatter.13
  706.6 68.1 reduce-scatter.11
  778.3 66.1 reduce-scatter.15
  846.5 98.8 all-gather.11
Sparse Core Ops, SparseCore 1:
  165.2 30.2 all-gather.7
  196.8 29.4 all-gather.9
